TPU v7x, 128 devices: a whole 4x4x4 slice. The times are simulated.
128 devices in a mesh: dom: 4 (over y_lo, core), cell: 32 (over x, y_hi, z).
Axes of the slice: x: 4, y: 4 (y_hi: 2, y_lo: 2; y = y_hi * 2 + y_lo), z: 4, core: 2. Of those that a mesh axis runs over, the one named last changes fastest.
Arguments:
- particles: float32 [512, 262144], P('dom', 'cell'), may hold values from -20 to 20
- gradients: float32 [512, 262144], P('dom', 'cell'), may hold values from -0.0034179688 to 0.0034179688
- width: float32 [1], replicated, may hold values from 655360 to 917504
- step_size: float32 [1], replicated, may hold values from 262144 to 524288
Outputs:
- moved: float32 [512, 262144], P('dom', 'cell')
All inputs are finite; a program needn't handle non-finite values.
Results may differ from a plain program's by a relative error of at most 0.000068.
Values sent between devices are 32-bit elements; how exact they have to be, the bound alone decides.
A program may use at most 128 MiB of HBM per device.

v0:
```python
import jax
import jax.numpy as jnp
from jax import lax
from jax.sharding import PartitionSpec as P


def inner_rows(left_rows, right_rows):
    return lax.dot_general(
        left_rows,
        right_rows,
        (((1,), (1,)), ((), ())),
        precision=lax.Precision.HIGHEST,
        preferred_element_type=jnp.float32,
    )


def on_device(particles, gradients, width, step_size):
    inv_band = 1.0 / width[0]
    sq_norms = jnp.sum(particles * particles, axis=1)
    all_rows = lax.all_gather(particles, "dom", axis=0, tiled=True)
    local_inner = inner_rows(particles, all_rows)
    all_norms = jnp.sum(all_rows * all_rows, axis=1)
    summed_inner, summed_own, summed_all = lax.psum((local_inner, sq_norms, all_norms), "cell")
    distance = summed_own[:, None] + summed_all[None, :] - 2.0 * summed_inner
    kernel = jnp.exp(-distance * inv_band)
    rowsum = jnp.sum(kernel, axis=1)
    shifted = gradients - 2.0 * inv_band * particles
    attracted = jnp.dot(
        kernel,
        lax.all_gather(shifted, "dom", axis=0, tiled=True),
        precision=lax.Precision.HIGHEST,
        preferred_element_type=jnp.float32,
    )
    velocity = (attracted + 2.0 * inv_band * particles * rowsum[:, None]) / kernel.shape[1]
    return particles + step_size[0] * velocity


def solution(mesh):
    in_specs = (P("dom", "cell"), P("dom", "cell"), P(), P())
    out_specs = P("dom", "cell")
    return jax.shard_map(
        on_device, mesh=mesh, in_specs=in_specs, out_specs=out_specs, check_vma=False
    )
```

profile of v0, /device:TPU:2, one launch (start us, length us, event | category | flops | bytes accessed | tf_op | source)
XLA Modules:
  0.0 706.8 jit_solution(2390411532301664047)
XLA Ops:
  6.5 0.0 all-gather.3.cloned.1.call-start
  6.5 0.7 all-gather.3.cloned.1.call-update
  7.3 0.0 all-reduce.3.cloned.1.call-start
  8.0 152.8 %all-gather.3.cloned.1.call-done = f32[512,8192]{1,0:T(8,128)} async-done(((f32[128,8192]{1,0:T(8,128)}), f32[512,8192]{1,0:T(8,128)}) %all-gather.3.cloned.1.call-update) | async-done | bytes 16777232 | tf_op jit(solution)/shard_map/all_gather | solution.py:20
  160.8 22.2 %fusion.8 = f32[128,512]{1,0:T(8,128)} fusion(f32[128,8192]{1,0:T(8,128)} %param.4, f32[512,8192]{1,0:T(8,128)} %all-gather.3.cloned.1.call-done), kind=kOutput, calls=%fused_computation.13 | convolution fusion | flops 6442450944 | bytes 21233664 | tf_op jit(solution)/shard_map/dot_general | solution.py:8
  183.0 0.0 all-reduce.3.cloned.1.call-update
  183.0 0.0 all-gather.5.cloned.1.call-start
  183.1 6.2 multiply_reduce_fusion.1
  189.3 0.0 all-gather.5.cloned.1.call-update
  189.9 7.0 multiply_reduce_fusion
  196.9 84.8 %all-reduce = (f32[512]{0:T(512)S(1)}, f32[128]{0:T(128)S(1)}) all-reduce(f32[512]{0:T(512)S(1)} %multiply_reduce_fusion, f32[128]{0:T(128)S(1)} %get-tuple-element.7), channel_id=1, replica_groups=mesh['dom'=4,'cell'=32] {'cell'}, use_global_device_ids=true, to_apply=%region_3.0 | all-reduce | flops 640 | bytes 5120 | tf_op jit(solution)/shard_map/psum | solution.py:23
  281.7 241.1 %all-reduce.3.cloned.1.call-done = f32[128,512]{1,0:T(8,128)} async-done(((f32[128,512]{1,0:T(8,128)}), f32[128,512]{1,0:T(8,128)}) %all-reduce.3.cloned.1.call-update) | async-done | bytes 262160 | tf_op jit(solution)/shard_map/psum | solution.py:23
  522.8 1.2 fusion.2
  524.0 161.6 %all-gather.5.cloned.1.call-done = f32[512,8192]{1,0:T(8,128)} async-done(((f32[128,8192]{1,0:T(8,128)}), f32[512,8192]{1,0:T(8,128)}) %all-gather.5.cloned.1.call-update) | async-done | bytes 16777232 | tf_op jit(solution)/shard_map/all_gather | solution.py:30
  685.6 14.7 %fusion.1 = f32[128,8192]{1,0:T(8,128)} fusion(f32[128,8192]{1,0:T(8,128)} %param.4, f32[512,8192]{1,0:T(8,128)} %all-gather.5.cloned.1.call-done, f32[]{:T(128)} %bitcast.1, f32[128]{0:T(128)S(1)} %fusion.2, f32[]{:T(128)S(6)} %mul.54, f32[128,512]{1,0:T(8,128)} %all-reduce.3.cloned.1.call-done, f32[]{:T(128)} %bitcast, f32[512]{0:T(512)S(1)} %get-tuple-element.5, ...), kind=kOutput, calls=%fused_computation.3 | convolution fusion | flops 6448021504 | bytes 25431052 | tf_op jit(solution)/shard_map/dot_general | solution.py:28
Async XLA Ops:
  6.5 154.3 %all-gather.3.cloned.1.call-start = ((), (), s32[]{:S(2)}) async-start(), calls=%async_computation | async-start | bytes 20971520 | tf_op jit(solution)/shard_map/all_gather | solution.py:20
  7.3 515.5 %all-reduce.3.cloned.1.call-start = ((), (), s32[]{:S(2)}) async-start(), calls=%async_computation.1 | async-start | bytes 524288 | tf_op jit(solution)/shard_map/psum | solution.py:23
  183.0 502.6 %all-gather.5.cloned.1.call-start = ((), (), s32[]{:S(2)}) async-start(), calls=%async_computation.2 | async-start | bytes 20971520 | tf_op jit(solution)/shard_map/all_gather | solution.py:30
Sparse Core Ops, SparseCore 0:
  9.0 151.7 all-gather.2
  183.1 339.6 all-reduce.2
  524.6 160.9 all-gather.4
where the time goes:
time: 710 us; the launch traced here: 707 us
  waiting for transfers between devices  556 us (78%)
  blocking collectives  84.8 us (12%)
  matrix products  36.9 us (5%)
  between operations  14.4 us (2%)
  other arithmetic  14.3 us (2%)
    psum x1, waiting for transfers between devices, on_device(): lax.psum((local_inner, sq_norms, all_norms), 'cell')  241 us
    all_gather x1, waiting for transfers between devices, on_device(): lax.all_gather(shifted, 'dom', axis=0, tiled=True)  162 us
    all_gather x1, waiting for transfers between devices, on_device(): all_rows = lax.all_gather(particles, 'dom', axis=0, tiled=True)  153 us
    psum x1, blocking collectives, on_device(): lax.psum((local_inner, sq_norms, all_norms), 'cell')  84.8 us
    dot_general x1, matrix products, inner_rows(): lax.dot_general(left_rows, right_rows, (((1,), (1,)), ((), ())), precisio...  22.2 us
    dot_general x1, matrix products, on_device(): jnp.dot(kernel, lax.all_gather(shifted, 'dom', axis=0, tiled=True), preci...  14.7 us
  transfers between devices with their start and end apart: 3, of which 3 were waited for; matrix products, arithmetic and copies ran while one was open for 2% of the time, Pallas kernels for 0%

commit v1 on v0

v1 whole, which is shorter than its diff:
```python
import functools

import jax
import jax.numpy as jnp
from jax import lax
from jax.experimental import pallas as pl
from jax.experimental.pallas import tpu as pltpu
from jax.sharding import PartitionSpec as P

MESH = pl.DeviceIdType.MESH
HIGHEST = lax.Precision.HIGHEST
NX, NYH, NZ = 4, 2, 4
GRAM_PARTS = 4
STEP_PARTS = 16
EARLY_PARTS = 6


def kernel(
    dims,
    width_ref,
    step_ref,
    particles,
    gradients,
    moved,
    x_own,
    s_own,
    x_gram,
    x_chip,
    s_all,
    result,
    part,
    sum_core,
    sum_x,
    sum_z,
    sum_y,
    inner,
    weights,
    load_sem,
    x_send,
    x_recv,
    xc_sem,
    ss_sem,
    s_send,
    s_recv,
    red_sem,
    own_sem,
    out_send,
    out_recv,
):
    rows, cells, nx, nz = dims
    every = 4 * rows
    half, quarter = cells // 2, cells // 4
    gram_cols, step_cols = quarter // GRAM_PARTS, half // STEP_PARTS
    dom, cell = lax.axis_index("dom"), lax.axis_index("cell")
    hi, lo = dom // 2, lax.rem(dom, 2)
    cx, cy, cz = cell // (NYH * nz), lax.rem(cell // nz, NYH), lax.rem(cell, nz)

    def cell_of(x, y, z):
        return (x * NYH + y) * nz + z

    sibling = (hi * 2 + 1 - lo, cell)
    across = [((1 - hi) * 2, cell), ((1 - hi) * 2 + 1, cell)]
    along_x = [lax.rem(cx + d, nx) for d in range(1, nx)]
    along_z = [lax.rem(cz + d, nz) for d in range(1, nz)]
    x_peers = [(dom, cell_of(x, cy, cz)) for x in along_x]
    z_peers = [(dom, cell_of(cx, cy, z)) for z in along_z]
    y_near = ((1 - hi) * 2 + lo, cell_of(cx, 1 - cy, cz))
    y_pair = ((1 - hi) * 2 + lo, cell)

    def send(src, dst, sems, to):
        return pltpu.make_async_remote_copy(
            src_ref=src,
            dst_ref=dst,
            send_sem=sems[0],
            recv_sem=sems[1],
            device_id=to,
            device_id_type=MESH,
        )

    def rows_of(index, count):
        return pl.ds(pl.multiple_of(index, count), count)

    def cols_of(index, count):
        return pl.ds(pl.multiple_of(index, count), count)

    my_rows = rows_of(dom * rows, rows)
    loads = [
        pltpu.make_async_copy(particles, x_own, load_sem.at[0]),
        pltpu.make_async_copy(gradients, s_own, load_sem.at[1]),
        pltpu.make_async_copy(
            particles.at[:, cols_of(half * lo + quarter * hi, quarter)],
            x_gram.at[my_rows],
            load_sem.at[2],
        ),
        pltpu.make_async_copy(
            particles.at[:, cols_of(half * lo, half)],
            x_chip.at[rows_of(lo * rows, rows)],
            load_sem.at[3],
        ),
    ]
    for load in loads:
        load.start()

    barrier = pltpu.get_barrier_semaphore()
    greeted = [sibling, *across, *x_peers, *z_peers, y_near]
    for peer in greeted:
        pl.semaphore_signal(barrier, inc=1, device_id=peer, device_id_type=MESH)
    pl.semaphore_wait(barrier, len(greeted))

    def gram_copy(slot, c):
        to = (across + [sibling])[slot]
        to_hi, to_lo = (hi, 1 - lo) if slot == 2 else (1 - hi, slot)
        start = half * to_lo + quarter * to_hi + gram_cols * c
        sem = lo if slot < 2 else 2
        return pltpu.make_async_remote_copy(
            src_ref=particles.at[:, cols_of(start, gram_cols)],
            dst_ref=x_gram.at[my_rows, cols_of(gram_cols * c, gram_cols)],
            send_sem=x_send.at[slot, c],
            recv_sem=x_recv.at[sem, c],
            device_id=to,
            device_id_type=MESH,
        )

    def gram_recv(sem, c):
        block = x_gram.at[pl.ds(0, rows), cols_of(gram_cols * c, gram_cols)]
        return pltpu.make_async_copy(block, block, x_recv.at[sem, c])

    for c in range(GRAM_PARTS):
        for slot in range(3):
            gram_copy(slot, c).start()
    x_swap = send(
        particles.at[:, cols_of(half * (1 - lo), half)],
        x_chip.at[rows_of(lo * rows, rows)],
        (xc_sem.at[0], xc_sem.at[1]),
        sibling,
    )
    x_swap.start()

    inv_band = 1.0 / width_ref[0]
    loads[0].wait()
    loads[1].wait()

    @pl.loop(0, STEP_PARTS * 2)
    def _(u):
        cols = cols_of(u * step_cols, step_cols)
        s_own[:, cols] = s_own[:, cols] - 2.0 * inv_band * x_own[:, cols]

    def step_copy(slot, u):
        return pltpu.make_async_remote_copy(
            src_ref=s_own.at[:, cols_of(half * slot + step_cols * u, step_cols)],
            dst_ref=s_all.at[my_rows, cols_of(step_cols * u, step_cols)],
            send_sem=s_send.at[slot, u],
            recv_sem=s_recv.at[lo, u],
            device_id=across[slot],
            device_id_type=MESH,
        )

    def step_recv(sem, u):
        block = s_all.at[pl.ds(0, rows), cols_of(step_cols * u, step_cols)]
        return pltpu.make_async_copy(block, block, s_recv.at[sem, u])

    @pl.loop(0, EARLY_PARTS)
    def _(u):
        for slot in range(2):
            step_copy(slot, u).start()

    s_swap = send(
        s_own.at[:, cols_of(half * (1 - lo), half)],
        s_all.at[my_rows],
        (ss_sem.at[0], ss_sem.at[1]),
        sibling,
    )
    s_swap.start()
    s_keep = pltpu.make_async_copy(
        s_own.at[:, cols_of(half * lo, half)], s_all.at[my_rows], load_sem.at[4]
    )
    s_keep.start()

    loads[2].wait()
    part[...] = jnp.zeros_like(part)

    @pl.loop(0, GRAM_PARTS)
    def _(c):
        for sem in range(3):
            if sem == 2:
                gram_recv(2, c).wait()
            else:
                gram_recv(sem, c).wait()
        block = x_gram[:, cols_of(gram_cols * c, gram_cols)]
        part[...] += lax.dot_general(
            block,
            block,
            (((1,), (1,)), ((), ())),
            precision=HIGHEST,
            preferred_element_type=jnp.float32,
        )

    n_core, n_x, n_z = every // 2, every // 2 // nx, every // 2 // nx // nz
    count = [0]

    def sems():
        k = count[0]
        count[0] += 1
        return red_sem.at[0, k], red_sem.at[1, k]

    swap = send(part.at[rows_of((1 - lo) * n_core, n_core)], sum_core, sems(), sibling)
    swap.start()
    swap.wait()
    sum_core[...] += part[rows_of(lo * n_core, n_core), :]

    copies = [
        send(sum_core.at[rows_of(x * n_x, n_x)], sum_x.at[d], sems(), peer)
        for d, (x, peer) in enumerate(zip(along_x, x_peers, strict=True))
    ]
    for copy in copies:
        copy.start()
    total = sum_core[rows_of(cx * n_x, n_x), :]
    for d, copy in enumerate(copies):
        copy.wait()
        total = total + sum_x[d]
    sum_x[nx - 1] = total

    copies = [
        send(sum_x.at[nx - 1, rows_of(z * n_z, n_z)], sum_z.at[d], sems(), peer)
        for d, (z, peer) in enumerate(zip(along_z, z_peers, strict=True))
    ]
    for copy in copies:
        copy.start()
    total = sum_x[nx - 1, rows_of(cz * n_z, n_z), :]
    for d, copy in enumerate(copies):
        copy.wait()
        total = total + sum_z[d]
    sum_y[0] = total
    swap = send(sum_y.at[0], sum_y.at[1], sems(), y_near)
    swap.start()
    swap.wait()
    sum_y[2] = sum_y[0] + sum_y[1]
    swap = send(sum_y.at[2], sum_y.at[3], sems(), y_pair)
    swap.start()

    @pl.loop(EARLY_PARTS, STEP_PARTS)
    def _(u):
        for slot in range(2):
            step_copy(slot, u).start()

    swap.wait()
    z_rows = rows_of(lo * n_core + cx * n_x + cz * n_z, n_z)
    inner[z_rows, :] = sum_y[2] + sum_y[3]
    copies = [send(inner.at[z_rows], inner.at[z_rows], sems(), peer) for peer in z_peers]
    for copy in copies:
        copy.start()
    for copy in copies:
        copy.wait()
    x_rows = rows_of(lo * n_core + cx * n_x, n_x)
    copies = [send(inner.at[x_rows], inner.at[x_rows], sems(), peer) for peer in x_peers]
    for copy in copies:
        copy.start()
    for copy in copies:
        copy.wait()
    core_rows = rows_of(lo * n_core, n_core)
    swap = send(inner.at[core_rows], inner.at[core_rows], sems(), sibling)
    swap.start()
    swap.wait()

    products = inner[...]
    i = lax.broadcasted_iota(jnp.int32, (every, every), 0)
    j = lax.broadcasted_iota(jnp.int32, (every, every), 1)
    all_norms = jnp.sum(jnp.where(i == j, products, 0.0), axis=0, keepdims=True)
    near = inner[rows_of(hi * 2 * rows, 2 * rows), :]
    i = lax.broadcasted_iota(jnp.int32, (2 * rows, every), 0) + hi * 2 * rows
    j = lax.broadcasted_iota(jnp.int32, (2 * rows, every), 1)
    own_norms = jnp.sum(jnp.where(i == j, near, 0.0), axis=1, keepdims=True)
    distance = own_norms + all_norms - 2.0 * near
    weights[...] = jnp.exp(-distance * inv_band)

    step_size = step_ref[0]
    pull = 2.0 * inv_band * jnp.sum(weights[...], axis=1, keepdims=True)
    loads[3].wait()
    x_swap.wait()
    s_swap.wait()
    s_keep.wait()

    def out_own(u):
        cols = cols_of(step_cols * u, step_cols)
        return pltpu.make_async_copy(
            result.at[rows_of(lo * rows, rows), cols],
            moved.at[:, cols_of(half * lo + step_cols * u, step_cols)],
            own_sem.at[u],
        )

    def out_swap(u):
        cols = cols_of(step_cols * u, step_cols)
        return send(
            result.at[rows_of((1 - lo) * rows, rows), cols],
            moved.at[:, cols_of(half * lo + step_cols * u, step_cols)],
            (out_send.at[u], out_recv.at[u]),
            sibling,
        )

    @pl.loop(0, STEP_PARTS)
    def _(u):
        for sem in range(2):
            step_recv(sem, u).wait()
        cols = cols_of(step_cols * u, step_cols)
        attracted = jnp.dot(
            weights[...],
            s_all[:, cols],
            precision=HIGHEST,
            preferred_element_type=jnp.float32,
        )
        x = x_chip[:, cols]
        result[:, cols] = x + step_size * ((attracted + pull * x) * (1.0 / every))
        out_own(u).start()
        out_swap(u).start()

    @pl.loop(0, STEP_PARTS)
    def _(u):
        for slot in range(2):
            step_copy(slot, u).wait_send()
        out_own(u).wait()
        out_swap(u).wait()

    @pl.loop(0, GRAM_PARTS)
    def _(c):
        for slot in range(3):
            gram_copy(slot, c).wait_send()


def on_device(dims, width, step_size, particles, gradients):
    rows, cells, nx, nz = dims
    every, half = 4 * rows, cells // 2
    n_core = every // 2
    n_x = n_core // nx
    n_z = n_x // nz
    f32 = jnp.float32
    sem = pltpu.SemaphoreType.DMA
    messages = 4 + 2 * (nx - 1) + 2 * (nz - 1)
    return pl.pallas_call(
        functools.partial(kernel, dims),
        out_shape=jax.ShapeDtypeStruct((rows, cells), f32),
        in_specs=[pl.BlockSpec(memory_space=pltpu.SMEM)] * 2 + [pl.BlockSpec(memory_space=pl.ANY)] * 2,
        out_specs=pl.BlockSpec(memory_space=pl.ANY),
        scratch_shapes=[
            pltpu.VMEM((rows, cells), f32),
            pltpu.VMEM((rows, cells), f32),
            pltpu.VMEM((every, cells // 4), f32),
            pltpu.VMEM((2 * rows, half), f32),
            pltpu.VMEM((every, half), f32),
            pltpu.VMEM((2 * rows, half), f32),
            pltpu.VMEM((every, every), f32),
            pltpu.VMEM((n_core, every), f32),
            pltpu.VMEM((nx, n_x, every), f32),
            pltpu.VMEM((nz, n_z, every), f32),
            pltpu.VMEM((4, n_z, every), f32),
            pltpu.VMEM((every, every), f32),
            pltpu.VMEM((2 * rows, every), f32),
            sem((5,)),
            sem((3, GRAM_PARTS)),
            sem((3, GRAM_PARTS)),
            sem((2,)),
            sem((2,)),
            sem((2, STEP_PARTS)),
            sem((2, STEP_PARTS)),
            sem((2, messages)),
            sem((STEP_PARTS,)),
            sem((STEP_PARTS,)),
            sem((STEP_PARTS,)),
        ],
        compiler_params=pltpu.CompilerParams(
            collective_id=0, has_side_effects=True, vmem_limit_bytes=60 * 2**20
        ),
        cost_estimate=pl.CostEstimate(
            flops=4 * every * every * cells // 4,
            bytes_accessed=5 * 4 * rows * cells,
            transcendentals=2 * rows * every,
        ),
    )(width, step_size, particles, gradients)


def solution(mesh):
    def step(particles, gradients, width, step_size):
        rows, cells = particles.shape
        nz = NZ if mesh.shape["cell"] == NX * NYH * NZ else 1
        nx = mesh.shape["cell"] // NYH // nz
        return on_device((rows, cells, nx, nz), width, step_size, particles, gradients)

    in_specs = (P("dom", "cell"), P("dom", "cell"), P(), P())
    out_specs = P("dom", "cell")
    return jax.shard_map(step, mesh=mesh, in_specs=in_specs, out_specs=out_specs, check_vma=False)
```

time: 710 us -> 152 us (0.21)
  waiting for transfers between devices: 556 us -> 0 us
  Pallas kernels: 0 us -> 145 us
  blocking collectives: 84.8 us -> 0 us
  matrix products: 36.9 us -> 0 us
  other arithmetic: 14.3 us -> 0 us
  between operations: 14.4 us -> 1.3 us
    all_gather x2 -> x0, waiting for transfers between devices: 314 us -> none  [the longest x1 162 us: on_device(): lax.all_gather(shifted, 'dom', axis=0, tiled=True)]
    psum x1 -> x0, waiting for transfers between devices: 241 us -> none  [on_device(): lax.psum((local_inner, sq_norms, all_norms), 'cell')]
    pallas_call x0 -> x1, Pallas kernels: none -> 145 us  [on_device(): pl.pallas_call(functools.partial(kernel, dims), out_shape=jax.ShapeDtypeS...]
    psum x1 -> x0, blocking collectives: 84.8 us -> none  [on_device(): lax.psum((local_inner, sq_norms, all_norms), 'cell')]
    dot_general x2 -> x0, matrix products: 36.9 us -> none  [the longest x1 22.2 us: inner_rows(): lax.dot_general(left_rows, right_rows, (((1,), (1,)), ((), ())), precisio...]
    reduce_sum x3 -> x0, other arithmetic: 14.3 us -> none  [the longest x1 6.98 us: on_device(): all_norms = jnp.sum(all_rows * all_rows, axis=1)]
  transfers between devices with their start and end apart: 3 -> 0, of which waited for: 3 -> 0; matrix products, arithmetic and copies ran while one was open for 2% -> 0% of each run, Pallas kernels for 0% -> 0%
where the time goes in v1:
time: 152 us; the launch traced here: 151 us
  Pallas kernels  145 us (95%)
  local copies, waits for them, and re-layouts  4.61 us (3%)
    pallas_call x1, Pallas kernels, on_device(): pl.pallas_call(functools.partial(kernel, dims), out_shape=jax.ShapeDtypeS...  145 us
    unnamed x1, local copies, waits for them, and re-layouts  4.61 us

profile of v1, /device:TPU:2, one launch (start us, length us, event | category | flops | bytes accessed | tf_op | source)
XLA Modules:
  0.0 150.9 jit_solution(9383388943949599641)
XLA Ops:
  1.3 145.0 %shard_map.46 = f32[128,8192]{1,0:T(8,128)} custom-call(f32[1]{0:T(128)S(6)} %copy.6.width_ref, f32[1]{0:T(128)S(6)} %copy.7.step_ref, f32[128,8192]{1,0:T(8,128)} %particles.1, f32[128,8192]{1,0:T(8,128)} %gradients.1), custom_call_target="tpu_custom_call" | custom-call | flops 2147483648 | bytes 20971520 | tf_op jit(solution)/shard_map/pallas_call | solution.py:338
  146.3 4.6 %copy.8 = f32[128,8192]{1,0:T(8,128)} copy(f32[128,8192]{1,0:T(8,128)} %shard_map.46) | data formatting | bytes 8388608

commit v2 on v1

v2 whole, which is shorter than its diff:
```python
import functools

import jax
import jax.numpy as jnp
from jax import lax
from jax.experimental import pallas as pl
from jax.experimental.pallas import tpu as pltpu
from jax.sharding import PartitionSpec as P

MESH = pl.DeviceIdType.MESH
HIGHEST = lax.Precision.HIGHEST
NX, NYH, NZ = 4, 2, 4
GRAM_PARTS = 4
STEP_PARTS = 16
MAIN_PARTS = STEP_PARTS - 1
EARLY_PARTS = 6


def kernel(
    dims,
    width_hbm,
    step_hbm,
    particles,
    gradients,
    moved,
    x_own,
    s_own,
    x_gram,
    x_chip,
    s_all,
    result,
    product,
    far,
    part,
    sum_core,
    sum_x,
    sum_z,
    sum_y,
    inner,
    width_ref,
    step_ref,
    ready,
    load_sem,
    x_send,
    x_recv,
    xc_sem,
    ss_sem,
    s_send,
    s_recv,
    red_sem,
    out_send,
    out_recv,
    far_send,
    far_recv,
):
    rows, cells, nx, nz = dims
    every = 4 * rows
    half, quarter = cells // 2, cells // 4
    gram_cols, step_cols = quarter // GRAM_PARTS, half // STEP_PARTS
    dom, cell = lax.axis_index("dom"), lax.axis_index("cell")
    hi, lo = dom // 2, lax.rem(dom, 2)
    cx, cy, cz = cell // (NYH * nz), lax.rem(cell // nz, NYH), lax.rem(cell, nz)

    def cell_of(x, y, z):
        return (x * NYH + y) * nz + z

    sibling = (hi * 2 + 1 - lo, cell)
    across = [((1 - hi) * 2, cell), ((1 - hi) * 2 + 1, cell)]
    along_x = [lax.rem(cx + d, nx) for d in range(1, nx)]
    along_z = [lax.rem(cz + d, nz) for d in range(1, nz)]
    x_peers = [(dom, cell_of(x, cy, cz)) for x in along_x]
    z_peers = [(dom, cell_of(cx, cy, z)) for z in along_z]
    y_near = ((1 - hi) * 2 + lo, cell_of(cx, 1 - cy, cz))
    y_pair = ((1 - hi) * 2 + lo, cell)

    def send(src, dst, sems, to):
        return pltpu.make_async_remote_copy(
            src_ref=src,
            dst_ref=dst,
            send_sem=sems[0],
            recv_sem=sems[1],
            device_id=to,
            device_id_type=MESH,
        )

    def rows_of(index, count):
        return pl.ds(pl.multiple_of(index, count), count)

    def cols_of(index, count):
        return pl.ds(pl.multiple_of(index, count), count)

    def signal(sem, to):
        pl.semaphore_signal(sem, inc=1, device_id=to, device_id_type=MESH)

    barrier = pltpu.get_barrier_semaphore()
    signal(barrier, across[0])

    @pl.when(lo == 1)
    def _():
        signal(barrier, sibling)

    my_rows = rows_of(dom * rows, rows)
    loads = [
        pltpu.make_async_copy(particles, x_own, load_sem.at[0]),
        pltpu.make_async_copy(gradients, s_own, load_sem.at[1]),
        pltpu.make_async_copy(
            particles.at[:, cols_of(half * lo + quarter * hi, quarter)],
            x_gram.at[my_rows],
            load_sem.at[2],
        ),
        pltpu.make_async_copy(
            particles.at[:, cols_of(half * lo, half)],
            x_chip.at[rows_of(lo * rows, rows)],
            load_sem.at[3],
        ),
        pltpu.make_async_copy(width_hbm, width_ref, load_sem.at[5]),
        pltpu.make_async_copy(step_hbm, step_ref, load_sem.at[6]),
    ]
    for load in loads:
        load.start()

    @pl.when(lo == 0)
    def _():
        pl.semaphore_wait(barrier, 3)
        signal(ready, sibling)
        signal(ready, across[1])

    @pl.when(lo == 1)
    def _():
        for peer in [*x_peers, *z_peers, y_near]:
            signal(barrier, peer)
        pl.semaphore_wait(ready, 2)

    def gram_copy(slot, c):
        to = (across + [sibling])[slot]
        to_hi, to_lo = (hi, 1 - lo) if slot == 2 else (1 - hi, slot)
        start = half * to_lo + quarter * to_hi + gram_cols * c
        sem = lo if slot < 2 else 2
        return pltpu.make_async_remote_copy(
            src_ref=particles.at[:, cols_of(start, gram_cols)],
            dst_ref=x_gram.at[my_rows, cols_of(gram_cols * c, gram_cols)],
            send_sem=x_send.at[slot, c],
            recv_sem=x_recv.at[sem, c],
            device_id=to,
            device_id_type=MESH,
        )

    def gram_recv(sem, c):
        block = x_gram.at[pl.ds(0, rows), cols_of(gram_cols * c, gram_cols)]
        return pltpu.make_async_copy(block, block, x_recv.at[sem, c])

    for c in range(GRAM_PARTS):
        for slot in range(3):
            gram_copy(slot, c).start()
    x_swap = send(
        particles.at[:, cols_of(half * (1 - lo), half)],
        x_chip.at[rows_of(lo * rows, rows)],
        (xc_sem.at[0], xc_sem.at[1]),
        sibling,
    )
    x_swap.start()

    loads[4].wait()
    loads[5].wait()
    inv_band = 1.0 / width_ref[0, 0]
    loads[0].wait()
    loads[1].wait()

    @pl.loop(0, STEP_PARTS * 2)
    def _(u):
        cols = cols_of(u * step_cols, step_cols)
        s_own[:, cols] = s_own[:, cols] - 2.0 * inv_band * x_own[:, cols]

    def step_copy(slot, u):
        return pltpu.make_async_remote_copy(
            src_ref=s_own.at[:, cols_of(half * slot + step_cols * u, step_cols)],
            dst_ref=s_all.at[my_rows, cols_of(step_cols * u, step_cols)],
            send_sem=s_send.at[slot, u],
            recv_sem=s_recv.at[lo, u],
            device_id=across[slot],
            device_id_type=MESH,
        )

    def step_recv(sem, u):
        block = s_all.at[pl.ds(0, rows), cols_of(step_cols * u, step_cols)]
        return pltpu.make_async_copy(block, block, s_recv.at[sem, u])

    @pl.loop(0, EARLY_PARTS)
    def _(u):
        for slot in range(2):
            step_copy(slot, u).start()

    s_swap = send(
        s_own.at[:, cols_of(half * (1 - lo), half)],
        s_all.at[my_rows],
        (ss_sem.at[0], ss_sem.at[1]),
        sibling,
    )
    s_swap.start()
    s_keep = pltpu.make_async_copy(
        s_own.at[:, cols_of(half * lo, half)], s_all.at[my_rows], load_sem.at[4]
    )
    s_keep.start()

    loads[2].wait()
    part[...] = jnp.zeros_like(part)

    @pl.loop(0, GRAM_PARTS)
    def _(c):
        for sem in range(3):
            if sem == 2:
                gram_recv(2, c).wait()
            else:
                gram_recv(sem, c).wait()
        block = x_gram[:, cols_of(gram_cols * c, gram_cols)]
        part[...] += lax.dot_general(
            block,
            block,
            (((1,), (1,)), ((), ())),
            precision=HIGHEST,
            preferred_element_type=jnp.float32,
        )

    n_x, n_z, n_y = every // nx, every // nx // nz, every // nx // nz // 2
    count = [0]

    def sems():
        k = count[0]
        count[0] += 1
        return red_sem.at[0, k], red_sem.at[1, k]

    def later_parts():
        @pl.loop(EARLY_PARTS, MAIN_PARTS)
        def _(u):
            for slot in range(2):
                step_copy(slot, u).start()

    to_core = send(part, sum_core, sems(), sibling)
    from_core = send(inner, inner, sems(), sibling)

    @pl.when(lo == 0)
    def _():
        to_core.start()
        to_core.wait_send()
        later_parts()
        from_core.wait_recv()

    @pl.when(lo == 1)
    def _():
        pl.semaphore_wait(barrier, len(x_peers) + len(z_peers) + 1)
        to_core.wait_recv()
        sum_core[...] += part[...]
        copies = [
            send(sum_core.at[rows_of(x * n_x, n_x)], sum_x.at[d], sems(), peer)
            for d, (x, peer) in enumerate(zip(along_x, x_peers, strict=True))
        ]
        for copy in copies:
            copy.start()
        total = sum_core[rows_of(cx * n_x, n_x), :]
        for d, copy in enumerate(copies):
            copy.wait()
            total = total + sum_x[d]
        sum_x[nx - 1] = total

        copies = [
            send(sum_x.at[nx - 1, rows_of(z * n_z, n_z)], sum_z.at[d], sems(), peer)
            for d, (z, peer) in enumerate(zip(along_z, z_peers, strict=True))
        ]
        for copy in copies:
            copy.start()
        total = sum_x[nx - 1, rows_of(cz * n_z, n_z), :]
        for d, copy in enumerate(copies):
            copy.wait()
            total = total + sum_z[d]
        sum_z[nz - 1] = total

        swap = send(sum_z.at[nz - 1, rows_of((1 - cy) * n_y, n_y)], sum_y.at[0], sems(), y_near)
        swap.start()
        swap.wait()
        sum_y[1] = sum_y[0] + sum_z[nz - 1, rows_of(cy * n_y, n_y), :]
        swap = send(sum_y.at[1], sum_y.at[2], sems(), y_pair)
        swap.start()
        later_parts()
        swap.wait()
        y_rows = rows_of(cx * n_x + cz * n_z + cy * n_y, n_y)
        z_rows = rows_of(cx * n_x + cz * n_z, n_z)
        x_rows = rows_of(cx * n_x, n_x)
        inner[y_rows, :] = sum_y[1] + sum_y[2]
        for block, peers in ((y_rows, [y_near]), (z_rows, z_peers), (x_rows, x_peers)):
            copies = [send(inner.at[block], inner.at[block], sems(), peer) for peer in peers]
            for copy in copies:
                copy.start()
            for copy in copies:
                copy.wait()
        from_core.start()
        from_core.wait_send()

    products = inner[...]
    i = lax.broadcasted_iota(jnp.int32, (every, every), 0)
    j = lax.broadcasted_iota(jnp.int32, (every, every), 1)
    norms = jnp.where(i == j, products, 0.0)
    distance = (
        jnp.sum(norms, axis=1, keepdims=True)
        + jnp.sum(norms, axis=0, keepdims=True)
        - 2.0 * products
    )
    inner[...] = jnp.exp(-distance * inv_band)
    near_rows = rows_of(hi * 2 * rows, 2 * rows)
    far_rows = rows_of((1 - hi) * 2 * rows, 2 * rows)
    near_cols = cols_of(hi * 2 * rows, 2 * rows)

    def dot(left, right):
        return jnp.dot(left, right, precision=HIGHEST, preferred_element_type=jnp.float32)

    s_swap.wait()
    s_keep.wait()
    last = step_cols * MAIN_PARTS
    last_cols = pl.ds(last, step_cols)
    product[...] = dot(inner[far_rows, near_cols], s_all[near_rows, last_cols])
    far_copies = [
        send(product.at[pl.ds(slot * rows, rows)], far.at[lo], (far_send.at[slot], far_recv.at[lo]), across[slot])
        for slot in range(2)
    ]
    for copy in far_copies:
        copy.start()

    step_size = step_ref[0, 0]
    pull = 2.0 * inv_band * jnp.sum(inner[near_rows, :], axis=1, keepdims=True)
    loads[3].wait()
    x_swap.wait()

    def out_cols(u):
        return cols_of(half * lo + step_cols * u, step_cols)

    def out_swap(u):
        return send(
            result.at[rows_of((1 - lo) * rows, rows), cols_of(step_cols * u, step_cols)],
            moved.at[:, out_cols(u)],
            (out_send.at[u], out_recv.at[u]),
            sibling,
        )

    def finish(u, attracted):
        cols = cols_of(step_cols * u, step_cols)
        x = x_chip[:, cols]
        result[:, cols] = x + step_size * ((attracted + pull * x) * (1.0 / every))
        out_swap(u).start()
        moved[:, out_cols(u)] = result[rows_of(lo * rows, rows), cols]

    finish(MAIN_PARTS, dot(inner[near_rows, near_cols], s_all[near_rows, last_cols]))

    @pl.loop(0, MAIN_PARTS)
    def _(u):
        for sem in range(2):
            step_recv(sem, u).wait()
        finish(u, dot(inner[near_rows, :], s_all[:, cols_of(step_cols * u, step_cols)]))

    @pl.loop(0, MAIN_PARTS)
    def _(u):
        for slot in range(2):
            step_copy(slot, u).wait_send()

    @pl.loop(0, GRAM_PARTS)
    def _(c):
        for slot in range(3):
            gram_copy(slot, c).wait_send()

    @pl.loop(0, STEP_PARTS)
    def _(u):
        out_swap(u).wait()

    for slot in range(2):
        pltpu.make_async_copy(far.at[slot], far.at[slot], far_recv.at[slot]).wait()
        cols = pl.ds(half * slot + last, step_cols)
        moved[:, cols] = moved[:, cols] + step_size * (far[slot] * (1.0 / every))
    for copy in far_copies:
        copy.wait_send()


def on_device(dims, width, step_size, particles, gradients):
    rows, cells, nx, nz = dims
    every, half = 4 * rows, cells // 2
    n_x = every // nx
    n_z = n_x // nz
    f32 = jnp.float32
    sem = pltpu.SemaphoreType.DMA
    messages = 5 + 2 * (nx - 1) + 2 * (nz - 1)
    return pl.pallas_call(
        functools.partial(kernel, dims),
        out_shape=pltpu.VMEM((rows, cells), f32),
        in_specs=[pl.BlockSpec(memory_space=pltpu.HBM)] * 4,
        out_specs=pl.BlockSpec(memory_space=pltpu.VMEM),
        scratch_shapes=[
            pltpu.VMEM((rows, cells), f32),
            pltpu.VMEM((rows, cells), f32),
            pltpu.VMEM((every, cells // 4), f32),
            pltpu.VMEM((2 * rows, half), f32),
            pltpu.VMEM((every, half), f32),
            pltpu.VMEM((2 * rows, half), f32),
            pltpu.VMEM((2 * rows, half // STEP_PARTS), f32),
            pltpu.VMEM((2, rows, half // STEP_PARTS), f32),
            pltpu.VMEM((every, every), f32),
            pltpu.VMEM((every, every), f32),
            pltpu.VMEM((nx, n_x, every), f32),
            pltpu.VMEM((nz, n_z, every), f32),
            pltpu.VMEM((3, n_z // 2, every), f32),
            pltpu.VMEM((every, every), f32),
            pltpu.SMEM((1, 1), f32),
            pltpu.SMEM((1, 1), f32),
            pltpu.SemaphoreType.REGULAR,
            sem((7,)),
            sem((3, GRAM_PARTS)),
            sem((3, GRAM_PARTS)),
            sem((2,)),
            sem((2,)),
            sem((2, STEP_PARTS)),
            sem((2, STEP_PARTS)),
            sem((2, messages)),
            sem((STEP_PARTS,)),
            sem((STEP_PARTS,)),
            sem((2,)),
            sem((2,)),
        ],
        compiler_params=pltpu.CompilerParams(
            collective_id=0, has_side_effects=True, vmem_limit_bytes=52 * 2**20
        ),
        cost_estimate=pl.CostEstimate(
            flops=4 * every * every * cells // 4,
            bytes_accessed=5 * 4 * rows * cells,
            transcendentals=2 * rows * every,
        ),
    )(
        width.reshape(1, 1),
        step_size.reshape(1, 1),
        particles,
        gradients,
    )


def solution(mesh):
    def step(particles, gradients, width, step_size):
        rows, cells = particles.shape
        nz = NZ if mesh.shape["cell"] == NX * NYH * NZ else 1
        nx = mesh.shape["cell"] // NYH // nz
        return on_device((rows, cells, nx, nz), width, step_size, particles, gradients)

    in_specs = (P("dom", "cell"), P("dom", "cell"), P(), P())
    out_specs = P("dom", "cell")
    return jax.shard_map(step, mesh=mesh, in_specs=in_specs, out_specs=out_specs, check_vma=False)
```

time: 152 us -> 145 us (0.954)
  Pallas kernels: 145 us -> 139 us
  local copies, waits for them, and re-layouts: 4.61 us -> 2.02 us
    pallas_call x1, Pallas kernels: 145 us -> 139 us  [on_device(): pl.pallas_call(functools.partial(kernel, dims), out_shape=pltpu.VMEM((row...]
    unnamed x1, local copies, waits for them, and re-layouts: 4.61 us -> 2.02 us
where the time goes in v2:
time: 145 us; the launch traced here: 143 us
  Pallas kernels  139 us (96%)
  local copies, waits for them, and re-layouts  2.02 us (1%)
    pallas_call x1, Pallas kernels, on_device(): pl.pallas_call(functools.partial(kernel, dims), out_shape=pltpu.VMEM((row...  139 us

profile of v2, /device:TPU:2, one launch (start us, length us, event | category | flops | bytes accessed | tf_op | source)
XLA Modules:
  0.0 142.7 jit_solution(4357121372370683619)
XLA Ops:
  1.3 139.3 %shard_map.46 = f32[128,8192]{1,0:T(8,128)S(1)} custom-call(f32[1,1]{1,0:T(1,128)} %bitcast.2.width_hbm, f32[1,1]{1,0:T(1,128)} %bitcast.3.step_hbm, f32[128,8192]{1,0:T(8,128)} %particles.1, f32[128,8192]{1,0:T(8,128)} %gradients.1), custom_call_target="tpu_custom_call" | custom-call | flops 2147483648 | bytes 20971520 | tf_op jit(solution)/shard_map/pallas_call | solution.py:388
  140.6 2.0 %copy.6 = f32[128,8192]{1,0:T(8,128)} copy(f32[128,8192]{1,0:T(8,128)S(1)} %shard_map.46) | data formatting | bytes 8388608

commit v3 on v2

--- a/solution.py
+++ b/solution.py
@@ -92,12 +92,14 @@
     def signal(sem, to):
         pl.semaphore_signal(sem, inc=1, device_id=to, device_id_type=MESH)
 
+    cross_peers = [*x_peers, *z_peers, y_near]
     barrier = pltpu.get_barrier_semaphore()
-    signal(barrier, across[0])
-
-    @pl.when(lo == 1)
+    signal(barrier, y_pair)
+
+    @pl.when(lo == 0)
     def _():
-        signal(barrier, sibling)
+        for peer in cross_peers:
+            signal(barrier, peer)
 
     my_rows = rows_of(dom * rows, rows)
     loads = [
@@ -119,18 +121,6 @@
     for load in loads:
         load.start()
 
-    @pl.when(lo == 0)
-    def _():
-        pl.semaphore_wait(barrier, 3)
-        signal(ready, sibling)
-        signal(ready, across[1])
-
-    @pl.when(lo == 1)
-    def _():
-        for peer in [*x_peers, *z_peers, y_near]:
-            signal(barrier, peer)
-        pl.semaphore_wait(ready, 2)
-
     def gram_copy(slot, c):
         to = (across + [sibling])[slot]
         to_hi, to_lo = (hi, 1 - lo) if slot == 2 else (1 - hi, slot)
@@ -149,9 +139,24 @@
         block = x_gram.at[pl.ds(0, rows), cols_of(gram_cols * c, gram_cols)]
         return pltpu.make_async_copy(block, block, x_recv.at[sem, c])
 
+    @pl.when(lo == 1)
+    def _():
+        pl.semaphore_wait(barrier, 1)
+        for c in range(GRAM_PARTS):
+            gram_copy(1, c).start()
+        signal(barrier, sibling)
+        pl.semaphore_wait(ready, 1)
+
+    @pl.when(lo == 0)
+    def _():
+        pl.semaphore_wait(barrier, 2 + len(cross_peers))
+        signal(ready, sibling)
+        for c in range(GRAM_PARTS):
+            gram_copy(1, c).start()
+
     for c in range(GRAM_PARTS):
-        for slot in range(3):
-            gram_copy(slot, c).start()
+        gram_copy(0, c).start()
+        gram_copy(2, c).start()
     x_swap = send(
         particles.at[:, cols_of(half * (1 - lo), half)],
         x_chip.at[rows_of(lo * rows, rows)],
@@ -238,16 +243,15 @@
     to_core = send(part, sum_core, sems(), sibling)
     from_core = send(inner, inner, sems(), sibling)
 
-    @pl.when(lo == 0)
+    @pl.when(lo == 1)
     def _():
         to_core.start()
         to_core.wait_send()
         later_parts()
         from_core.wait_recv()
 
-    @pl.when(lo == 1)
+    @pl.when(lo == 0)
     def _():
-        pl.semaphore_wait(barrier, len(x_peers) + len(z_peers) + 1)
         to_core.wait_recv()
         sum_core[...] += part[...]
         copies = [

time: 145 us -> 144 us (level)
  no operation moved by 1% of the time
where the time goes in v3:
time: 144 us; the launch traced here: 142 us
  Pallas kernels  139 us (97%)
  local copies, waits for them, and re-layouts  2.02 us (1%)
    pallas_call x1, Pallas kernels, on_device(): pl.pallas_call(functools.partial(kernel, dims), out_shape=pltpu.VMEM((row...  139 us

profile of v3, /device:TPU:2, one launch (start us, length us, event | category | flops | bytes accessed | tf_op | source)
XLA Modules:
  0.0 141.9 jit_solution(10547138986173879184)
XLA Ops:
  1.3 138.6 %shard_map.46 = f32[128,8192]{1,0:T(8,128)S(1)} custom-call(f32[1,1]{1,0:T(1,128)} %bitcast.2.width_hbm, f32[1,1]{1,0:T(1,128)} %bitcast.3.step_hbm, f32[128,8192]{1,0:T(8,128)} %particles.1, f32[128,8192]{1,0:T(8,128)} %gradients.1), custom_call_target="tpu_custom_call" | custom-call | flops 2147483648 | bytes 20971520 | tf_op jit(solution)/shard_map/pallas_call | solution.py:392
  139.9 2.0 %copy.6 = f32[128,8192]{1,0:T(8,128)} copy(f32[128,8192]{1,0:T(8,128)S(1)} %shard_map.46) | data formatting | bytes 8388608

commit v4 on v3

--- a/solution.py
+++ b/solution.py
@@ -118,9 +118,6 @@
         pltpu.make_async_copy(width_hbm, width_ref, load_sem.at[5]),
         pltpu.make_async_copy(step_hbm, step_ref, load_sem.at[6]),
     ]
-    for load in loads:
-        load.start()
-
     def gram_copy(slot, c):
         to = (across + [sibling])[slot]
         to_hi, to_lo = (hi, 1 - lo) if slot == 2 else (1 - hi, slot)
@@ -142,9 +139,9 @@
     @pl.when(lo == 1)
     def _():
         pl.semaphore_wait(barrier, 1)
+        signal(barrier, sibling)
         for c in range(GRAM_PARTS):
             gram_copy(1, c).start()
-        signal(barrier, sibling)
         pl.semaphore_wait(ready, 1)
 
     @pl.when(lo == 0)
@@ -157,6 +154,8 @@
     for c in range(GRAM_PARTS):
         gram_copy(0, c).start()
         gram_copy(2, c).start()
+    for load in loads:
+        load.start()
     x_swap = send(
         particles.at[:, cols_of(half * (1 - lo), half)],
         x_chip.at[rows_of(lo * rows, rows)],
@@ -325,8 +324,16 @@
         send(product.at[pl.ds(slot * rows, rows)], far.at[lo], (far_send.at[slot], far_recv.at[lo]), across[slot])
         for slot in range(2)
     ]
-    for copy in far_copies:
-        copy.start()
+    @pl.when(lo == 1)
+    def _():
+        far_copies[0].start()
+        far_copies[1].start()
+
+    @pl.when(lo == 0)
+    def _():
+        far_copies[1].start()
+        far_copies[0].start()
+
 
     step_size = step_ref[0, 0]
     pull = 2.0 * inv_band * jnp.sum(inner[near_rows, :], axis=1, keepdims=True)

time: 144 us -> 143 us (level); the launches traced: 142 us -> 143 us
  no operation moved by 1% of the time
where the time goes in v4:
time: 143 us
  Pallas kernels  139 us (97%)
  local copies, waits for them, and re-layouts  2.02 us (1%)
    pallas_call x1, Pallas kernels, on_device(): pl.pallas_call(functools.partial(kernel, dims), out_shape=pltpu.VMEM((row...  139 us

profile of v4, /device:TPU:2, one launch (start us, length us, event | category | flops | bytes accessed | tf_op | source)
XLA Modules:
  0.0 142.8 jit_solution(15577165745491065302)
XLA Ops:
  1.3 139.5 %shard_map.46 = f32[128,8192]{1,0:T(8,128)S(1)} custom-call(f32[1,1]{1,0:T(1,128)} %bitcast.2.width_hbm, f32[1,1]{1,0:T(1,128)} %bitcast.3.step_hbm, f32[128,8192]{1,0:T(8,128)} %particles.1, f32[128,8192]{1,0:T(8,128)} %gradients.1), custom_call_target="tpu_custom_call" | custom-call | flops 2147483648 | bytes 20971520 | tf_op jit(solution)/shard_map/pallas_call | solution.py:399
  140.8 2.0 %copy.6 = f32[128,8192]{1,0:T(8,128)} copy(f32[128,8192]{1,0:T(8,128)S(1)} %shard_map.46) | data formatting | bytes 8388608

commit v5 on v4

--- a/solution.py
+++ b/solution.py
@@ -11,9 +11,9 @@
 HIGHEST = lax.Precision.HIGHEST
 NX, NYH, NZ = 4, 2, 4
 GRAM_PARTS = 4
-STEP_PARTS = 16
+STEP_PARTS = 8
 MAIN_PARTS = STEP_PARTS - 1
-EARLY_PARTS = 6
+EARLY_PARTS = 3
 
 
 def kernel(

time: 143 us -> 143 us (level)
  no operation moved by 1% of the time
where the time goes in v5:
time: 143 us; the launch traced here: 142 us
  Pallas kernels  139 us (97%)
  local copies, waits for them, and re-layouts  2.02 us (1%)
    pallas_call x1, Pallas kernels, on_device(): pl.pallas_call(functools.partial(kernel, dims), out_shape=pltpu.VMEM((row...  139 us

profile of v5, /device:TPU:2, one launch (start us, length us, event | category | flops | bytes accessed | tf_op | source)
XLA Modules:
  0.0 142.4 jit_solution(10397526303596706787)
XLA Ops:
  1.3 139.1 %shard_map.46 = f32[128,8192]{1,0:T(8,128)S(1)} custom-call(f32[1,1]{1,0:T(1,128)} %bitcast.2.width_hbm, f32[1,1]{1,0:T(1,128)} %bitcast.3.step_hbm, f32[128,8192]{1,0:T(8,128)} %particles.1, f32[128,8192]{1,0:T(8,128)} %gradients.1), custom_call_target="tpu_custom_call" | custom-call | flops 2147483648 | bytes 20971520 | tf_op jit(solution)/shard_map/pallas_call | solution.py:399
  140.4 2.0 %copy.6 = f32[128,8192]{1,0:T(8,128)} copy(f32[128,8192]{1,0:T(8,128)S(1)} %shard_map.46) | data formatting | bytes 8388608

commit v6 on v5

--- a/solution.py
+++ b/solution.py
@@ -212,10 +212,7 @@
     @pl.loop(0, GRAM_PARTS)
     def _(c):
         for sem in range(3):
-            if sem == 2:
-                gram_recv(2, c).wait()
-            else:
-                gram_recv(sem, c).wait()
+            gram_recv(sem, c).wait()
         block = x_gram[:, cols_of(gram_cols * c, gram_cols)]
         part[...] += lax.dot_general(
             block,
@@ -360,27 +357,29 @@
 
     finish(MAIN_PARTS, dot(inner[near_rows, near_cols], s_all[near_rows, last_cols]))
 
+    @pl.loop(0, GRAM_PARTS)
+    def _(c):
+        for slot in range(3):
+            gram_copy(slot, c).wait_send()
+
+    def leave(u):
+        for slot in range(2):
+            step_copy(slot, u).wait_send()
+        out_swap(u).wait()
+
     @pl.loop(0, MAIN_PARTS)
     def _(u):
         for sem in range(2):
             step_recv(sem, u).wait()
         finish(u, dot(inner[near_rows, :], s_all[:, cols_of(step_cols * u, step_cols)]))
 
-    @pl.loop(0, MAIN_PARTS)
-    def _(u):
-        for slot in range(2):
-            step_copy(slot, u).wait_send()
-
-    @pl.loop(0, GRAM_PARTS)
-    def _(c):
-        for slot in range(3):
-            gram_copy(slot, c).wait_send()
-
-    @pl.loop(0, STEP_PARTS)
-    def _(u):
-        out_swap(u).wait()
-
-    for slot in range(2):
+        @pl.when(u > 0)
+        def _():
+            leave(u - 1)
+
+    leave(MAIN_PARTS - 1)
+    out_swap(MAIN_PARTS).wait()
+    for slot in (1, 0):
         pltpu.make_async_copy(far.at[slot], far.at[slot], far_recv.at[slot]).wait()
         cols = pl.ds(half * slot + last, step_cols)
         moved[:, cols] = moved[:, cols] + step_size * (far[slot] * (1.0 / every))

time: 143 us -> 142 us (level)
  no operation moved by 1% of the time
where the time goes in v6:
time: 142 us
  Pallas kernels  139 us (98%)
  local copies, waits for them, and re-layouts  2.02 us (1%)
    pallas_call x1, Pallas kernels, on_device(): pl.pallas_call(functools.partial(kernel, dims), out_shape=pltpu.VMEM((row...  139 us

profile of v6, /device:TPU:2, one launch (start us, length us, event | category | flops | bytes accessed | tf_op | source)
XLA Modules:
  0.0 142.4 jit_solution(11642087802699880148)
XLA Ops:
  1.3 139.1 %shard_map.46 = f32[128,8192]{1,0:T(8,128)S(1)} custom-call(f32[1,1]{1,0:T(1,128)} %bitcast.2.width_hbm, f32[1,1]{1,0:T(1,128)} %bitcast.3.step_hbm, f32[128,8192]{1,0:T(8,128)} %particles.1, f32[128,8192]{1,0:T(8,128)} %gradients.1), custom_call_target="tpu_custom_call" | custom-call | flops 2147483648 | bytes 20971520 | tf_op jit(solution)/shard_map/pallas_call | solution.py:398
  140.4 2.0 %copy.6 = f32[128,8192]{1,0:T(8,128)} copy(f32[128,8192]{1,0:T(8,128)S(1)} %shard_map.46) | data formatting | bytes 8388608

commit v7 on v5

--- a/solution.py
+++ b/solution.py
@@ -12,7 +12,8 @@
 NX, NYH, NZ = 4, 2, 4
 GRAM_PARTS = 4
 STEP_PARTS = 8
-MAIN_PARTS = STEP_PARTS - 1
+LAST_PARTS = 2
+MAIN_PARTS = STEP_PARTS - LAST_PARTS
 EARLY_PARTS = 3
 
 
@@ -318,7 +319,8 @@
     s_swap.wait()
     s_keep.wait()
     last = step_cols * MAIN_PARTS
-    last_cols = pl.ds(last, step_cols)
+    last_count = step_cols * LAST_PARTS
+    last_cols = pl.ds(last, last_count)
     product[...] = dot(inner[far_rows, near_cols], s_all[near_rows, last_cols])
     far_copies = [
         send(product.at[pl.ds(slot * rows, rows)], far.at[lo], (far_send.at[slot], far_recv.at[lo]), across[slot])
@@ -358,7 +360,9 @@
         out_swap(u).start()
         moved[:, out_cols(u)] = result[rows_of(lo * rows, rows), cols]
 
-    finish(MAIN_PARTS, dot(inner[near_rows, near_cols], s_all[near_rows, last_cols]))
+    for u in range(MAIN_PARTS, STEP_PARTS):
+        part_cols = pl.ds(step_cols * u, step_cols)
+        finish(u, dot(inner[near_rows, near_cols], s_all[near_rows, part_cols]))
 
     @pl.loop(0, MAIN_PARTS)
     def _(u):
@@ -382,7 +386,7 @@
 
     for slot in range(2):
         pltpu.make_async_copy(far.at[slot], far.at[slot], far_recv.at[slot]).wait()
-        cols = pl.ds(half * slot + last, step_cols)
+        cols = pl.ds(half * slot + last, last_count)
         moved[:, cols] = moved[:, cols] + step_size * (far[slot] * (1.0 / every))
     for copy in far_copies:
         copy.wait_send()
@@ -408,8 +412,8 @@
             pltpu.VMEM((2 * rows, half), f32),
             pltpu.VMEM((every, half), f32),
             pltpu.VMEM((2 * rows, half), f32),
-            pltpu.VMEM((2 * rows, half // STEP_PARTS), f32),
-            pltpu.VMEM((2, rows, half // STEP_PARTS), f32),
+            pltpu.VMEM((2 * rows, half // STEP_PARTS * LAST_PARTS), f32),
+            pltpu.VMEM((2, rows, half // STEP_PARTS * LAST_PARTS), f32),
             pltpu.VMEM((every, every), f32),
             pltpu.VMEM((every, every), f32),
             pltpu.VMEM((nx, n_x, every), f32),

time: 143 us -> 143 us (level)
  no operation moved by 1% of the time
where the time goes in v7:
time: 143 us; the launch traced here: 142 us
  Pallas kernels  139 us (97%)
  local copies, waits for them, and re-layouts  2.02 us (1%)
    pallas_call x1, Pallas kernels, on_device(): pl.pallas_call(functools.partial(kernel, dims), out_shape=pltpu.VMEM((row...  139 us

profile of v7, /device:TPU:2, one launch (start us, length us, event | category | flops | bytes accessed | tf_op | source)
XLA Modules:
  0.0 142.5 jit_solution(15080320109889979333)
XLA Ops:
  1.3 139.1 %shard_map.46 = f32[128,8192]{1,0:T(8,128)S(1)} custom-call(f32[1,1]{1,0:T(1,128)} %bitcast.2.width_hbm, f32[1,1]{1,0:T(1,128)} %bitcast.3.step_hbm, f32[128,8192]{1,0:T(8,128)} %particles.1, f32[128,8192]{1,0:T(8,128)} %gradients.1), custom_call_target="tpu_custom_call" | custom-call | flops 2147483648 | bytes 20971520 | tf_op jit(solution)/shard_map/pallas_call | solution.py:403
  140.4 2.0 %copy.6 = f32[128,8192]{1,0:T(8,128)} copy(f32[128,8192]{1,0:T(8,128)S(1)} %shard_map.46) | data formatting | bytes 8388608

commit v8 on v5

--- a/solution.py
+++ b/solution.py
@@ -320,20 +320,28 @@
     last = step_cols * MAIN_PARTS
     last_cols = pl.ds(last, step_cols)
     product[...] = dot(inner[far_rows, near_cols], s_all[near_rows, last_cols])
-    far_copies = [
-        send(product.at[pl.ds(slot * rows, rows)], far.at[lo], (far_send.at[slot], far_recv.at[lo]), across[slot])
-        for slot in range(2)
-    ]
+    piece = step_cols // 2
+
+    def far_copy(slot, k):
+        cols = pl.ds(piece * k, piece)
+        return send(
+            product.at[pl.ds(slot * rows, rows), cols],
+            far.at[lo, :, cols],
+            (far_send.at[slot, k], far_recv.at[lo, k]),
+            across[slot],
+        )
+
+    @pl.when(lo == 0)
+    def _():
+        for k in range(2):
+            far_copy(1, k).start()
+            far_copy(0, k).start()
+
     @pl.when(lo == 1)
     def _():
-        far_copies[0].start()
-        far_copies[1].start()
-
-    @pl.when(lo == 0)
-    def _():
-        far_copies[1].start()
-        far_copies[0].start()
-
+        for k in range(2):
+            far_copy(0, k).start()
+            far_copy(1, k).start()
 
     step_size = step_ref[0, 0]
     pull = 2.0 * inv_band * jnp.sum(inner[near_rows, :], axis=1, keepdims=True)
@@ -381,11 +389,14 @@
         out_swap(u).wait()
 
     for slot in range(2):
-        pltpu.make_async_copy(far.at[slot], far.at[slot], far_recv.at[slot]).wait()
+        for k in range(2):
+            block = far.at[slot, :, pl.ds(piece * k, piece)]
+            pltpu.make_async_copy(block, block, far_recv.at[slot, k]).wait()
         cols = pl.ds(half * slot + last, step_cols)
         moved[:, cols] = moved[:, cols] + step_size * (far[slot] * (1.0 / every))
-    for copy in far_copies:
-        copy.wait_send()
+    for slot in range(2):
+        for k in range(2):
+            far_copy(slot, k).wait_send()
 
 
 def on_device(dims, width, step_size, particles, gradients):
@@ -429,8 +440,8 @@
             sem((2, messages)),
             sem((STEP_PARTS,)),
             sem((STEP_PARTS,)),
-            sem((2,)),
-            sem((2,)),
+            sem((2, 2)),
+            sem((2, 2)),
         ],
         compiler_params=pltpu.CompilerParams(
             collective_id=0, has_side_effects=True, vmem_limit_bytes=52 * 2**20

time: 143 us -> 143 us (level)
  no operation moved by 1% of the time
where the time goes in v8:
time: 143 us; the launch traced here: 142 us
  Pallas kernels  139 us (97%)
  local copies, waits for them, and re-layouts  2.02 us (1%)
    pallas_call x1, Pallas kernels, on_device(): pl.pallas_call(functools.partial(kernel, dims), out_shape=pltpu.VMEM((row...  139 us

profile of v8, /device:TPU:2, one launch (start us, length us, event | category | flops | bytes accessed | tf_op | source)
XLA Modules:
  0.0 142.4 jit_solution(9972875822641398259)
XLA Ops:
  1.3 139.1 %shard_map.46 = f32[128,8192]{1,0:T(8,128)S(1)} custom-call(f32[1,1]{1,0:T(1,128)} %bitcast.2.width_hbm, f32[1,1]{1,0:T(1,128)} %bitcast.3.step_hbm, f32[128,8192]{1,0:T(8,128)} %particles.1, f32[128,8192]{1,0:T(8,128)} %gradients.1), custom_call_target="tpu_custom_call" | custom-call | flops 2147483648 | bytes 20971520 | tf_op jit(solution)/shard_map/pallas_call | solution.py:410
  140.4 2.0 %copy.6 = f32[128,8192]{1,0:T(8,128)} copy(f32[128,8192]{1,0:T(8,128)S(1)} %shard_map.46) | data formatting | bytes 8388608
